TPU v7x, 128 devices: a whole 4x4x4 slice. The times are simulated.
128 devices in a mesh: grp: 8 (over x, core), blk: 16 (over y, z).
Axes of the slice: x: 4, y: 4, z: 4, core: 2. Of those that a mesh axis runs over, the one named last changes fastest.
Arguments:
- stamps: float32 [128, 128, 64, 128], P(('grp', 'blk')), may hold values from -1 to 1
- stamp_target: int32 [128, 128, 128], P(('grp', 'blk')), may hold values from 0 to 4095
- pair_counts: int32 [128, 128], P(('grp', 'blk')), may hold values from 0 to 128, as said below
- conductance: float32 [8, 32768], P(None, ('grp', 'blk')), may hold values from 4 to 12
- block_cols: int32 [16, 32768], P(None, ('grp', 'blk')), may hold values from 0 to 32767, as said below
- newton_residual: float32 [8, 32768], P(None, ('grp', 'blk')), may hold values from -30 to 30
Outputs:
- update: float32 [8, 32768], P(None, ('grp', 'blk'))
- jacobian_blocks: float32 [16, 8, 8, 32768], P(None, None, None, ('grp', 'blk'))
- preconditioned_rhs: float32 [8, 32768], P(None, ('grp', 'blk'))
Inputs may be any that keep to these rules, and one draw needn't show every extreme that they name: `stamp_target`: A stamp's target is its block slot times 256 plus its block row local to the owner. `pair_counts`: every device sends exactly 128 live blocks to itself and exactly 128 to the next device in the order of grp+blk (the last device to the first), and at most 32 to every other owner; one owner drawn from the seed receives exactly 32 from every device other than itself and the device before it. `block_cols`: slot 0 of block row n names n itself; slots 1 to 7 name rows of the same group of 4096 rows as n; over the 256 block rows of one device, the slots from 8 on name rows owned by each device exactly 16 times.
All inputs are finite; a program needn't handle non-finite values.
Results may differ from a plain program's by a relative error of at most 0.0003.
Values sent between devices are 32-bit elements; how exact they have to be, the bound alone decides.
A program may use at most 128 MiB of HBM per device.

v0:
```python
import jax
import jax.numpy as jnp
from jax import lax
from jax.sharding import Mesh
from jax.sharding import PartitionSpec as P

K = 16
KRYLOV = 5
SWEEPS = 2
GRP = ("grp_0", "grp_1")
BLK = ("blk_0", "blk_1")
GRP_BLK = ("grp_0", "grp_1", "blk_0", "blk_1")
EPS = 1e-06


def sent_together(arrays, axis, split_dim, concat_dim, along):
    columns = [a.reshape(*a.shape[:along], -1) for a in arrays]
    both = jnp.concatenate(columns, axis=along)
    result, at, done = (
        lax.all_to_all(both, axis, split_axis=split_dim, concat_axis=concat_dim, tiled=True),
        0,
        [],
    )
    for a, column in zip(arrays, columns):
        piece = result[..., at : at + column.shape[along]]
        done.append(piece.reshape(*piece.shape[:along], *a.shape[along:]))
        at += column.shape[along]
    return tuple(done)


def passed_along(block, axis, distance):
    devices = range(lax.axis_size(axis))
    route = [((i - distance) % len(devices), i) for i in devices]
    return lax.ppermute(block, axis, route)


def in_order(parts, dim):
    dims = list(parts.shape[1:])
    dims[dim] *= parts.shape[0]
    return jnp.moveaxis(parts, 0, dim).reshape(dims)


def copy_for_each(array, axis):
    length = lax.axis_size(axis)
    return lax.all_to_all(
        jnp.broadcast_to(array[None], (length, *array.shape)), axis, 0, 0, tiled=True
    )


def collect(array, axis, dim):
    return in_order(copy_for_each(array, axis), dim)


def all_blocks(array, axes, sequence):
    parts = array[None]
    for k in sequence:
        parts = lax.all_gather(parts, axes[k], axis=0, tiled=True)
    held = [lax.axis_size(axes[k]) for k in reversed(sequence)]
    parts = parts.reshape(*held, *array.shape)
    turned = sorted(range(len(sequence)), key=lambda place: sequence[len(sequence) - 1 - place])
    return parts.transpose(*turned, *range(len(sequence), parts.ndim)).reshape(-1, *array.shape)


def gathered_by_axis(array, axes, sequence, dim):
    return in_order(all_blocks(array, axes, sequence), dim)


def by_axis(array, axes):
    for axis in axes:
        array = lax.psum(array, axis)
    return array


def invert_blocks(diag):
    size = diag.shape[0]
    eye_mat = jnp.eye(size, dtype=jnp.float32)[:, :, None]
    inverse = eye_mat * jnp.ones_like(diag[:1])
    work = diag
    for pivot_row in range(size):
        scale = 1.0 / work[pivot_row, pivot_row]
        top_work = work[pivot_row] * scale
        top_inverse = inverse[pivot_row] * scale
        factor = work[:, pivot_row]
        work = work - factor[:, None, :] * top_work[None]
        inverse = inverse - factor[:, None, :] * top_inverse[None]
        work = work.at[pivot_row].set(top_work)
        inverse = inverse.at[pivot_row].set(top_inverse)
    return inverse


def solve_small(matrix, rhs_vector):
    count = matrix.shape[0]
    work, vector = (matrix, rhs_vector)
    for pivot_row in range(count):
        scale = 1.0 / work[pivot_row, pivot_row]
        top_work = work[pivot_row] * scale
        top_rhs = vector[pivot_row] * scale
        factor = work[:, pivot_row]
        work = work - factor[:, None] * top_work[None, :]
        vector = vector - factor * top_rhs
        work = work.at[pivot_row].set(top_work)
        vector = vector.at[pivot_row].set(top_rhs)
    return vector


def block_apply(inverse, vector):
    return jnp.einsum("abn,bn->an", inverse, vector, precision=lax.Precision.HIGHEST)


def couple(jacobian, picked):
    return jnp.einsum("kabn,bkn->an", jacobian, picked, precision=lax.Precision.HIGHEST)


def add_stamps(summed, values, targets, counts, offset, local_rows):
    slots = values.shape[2]
    slot_ids = offset + jnp.arange(slots, dtype=jnp.int32)
    live = slot_ids[None, :] < counts
    masked = jnp.where(live[:, None, :], values, 0.0)
    index_pairs = jnp.stack([targets // local_rows, targets % local_rows], axis=2).astype(jnp.int32)
    numbers = lax.ScatterDimensionNumbers(
        update_window_dims=(1,), inserted_window_dims=(0, 2), scatter_dims_to_operand_dims=(0, 2)
    )
    return lax.scatter_add(summed, index_pairs, masked, numbers)


def local(stamps, stamp_target, pair_counts, conductance, block_cols, newton_residual):
    grp_count = lax.axis_size(GRP)
    blk_count = lax.axis_size(BLK)
    devices = grp_count * blk_count
    local_rows = conductance.shape[1]
    capacity = stamps.shape[3]
    summed = jnp.zeros((K, 64, local_rows), jnp.float32)
    front = capacity // 4
    got_values, got_target, got_counts = (
        lax.all_to_all(stamps[:, :, :, :front], GRP_BLK, split_axis=1, concat_axis=0, tiled=True),
        *sent_together((stamp_target[:, :, :front], pair_counts), GRP_BLK, 1, 0, 2),
    )
    summed = add_stamps(
        summed,
        got_values.reshape(devices, 64, front),
        got_target.reshape(devices, front),
        got_counts,
        0,
        local_rows,
    )
    my_index = lax.axis_index(GRP_BLK)
    next_index = (my_index + 1) % devices
    own_values = lax.dynamic_index_in_dim(stamps[0], my_index, 0, keepdims=False)[:, front:]
    own_target = lax.dynamic_index_in_dim(stamp_target[0], my_index, 0, keepdims=False)[front:]
    own_count = lax.dynamic_index_in_dim(pair_counts[0], my_index, 0, keepdims=True)
    next_values = lax.dynamic_index_in_dim(stamps[0], next_index, 0, keepdims=False)[:, front:]
    next_target = lax.dynamic_index_in_dim(stamp_target[0], next_index, 0, keepdims=False)[front:]
    next_count = lax.dynamic_index_in_dim(pair_counts[0], next_index, 0, keepdims=True)
    prior_values, prior_target, prior_count = passed_along(
        (next_values, next_target, next_count), GRP_BLK, 1
    )
    tail_values = jnp.stack([own_values, prior_values], axis=0)
    tail_target = jnp.stack([own_target, prior_target], axis=0)
    tail_counts = jnp.stack([own_count, prior_count], axis=0)
    summed = add_stamps(summed, tail_values, tail_target, tail_counts, front, local_rows)
    jacobian = summed.reshape(K, 8, 8, local_rows)
    identity = jnp.eye(8, dtype=jnp.float32)
    jacobian = jacobian.at[0].add(identity[:, :, None] * conductance[:, None, :])
    inverse = invert_blocks(jacobian[0])
    group_rows = local_rows * blk_count
    group_start = lax.axis_index(GRP) * group_rows
    slot_ids = jnp.arange(K, dtype=jnp.int32)[:, None]
    near = (block_cols >= group_start) & (block_cols < group_start + group_rows) & (slot_ids >= 1)
    local_cols = jnp.clip(block_cols - group_start, 0, group_rows - 1)
    rhs_field = -newton_residual
    beta = jnp.sqrt(by_axis(jnp.sum(rhs_field * rhs_field), GRP_BLK) + EPS)
    basis = [rhs_field / beta]
    search = []
    hess = jnp.zeros((KRYLOV + 1, KRYLOV), jnp.float32)
    for krylov_step in range(KRYLOV):
        precondition_vector = basis[krylov_step]
        result = block_apply(inverse, precondition_vector)
        for sweep_index in range(SWEEPS):
            grouped = collect(result, BLK, 1)
            precondition_picked = jnp.where(near[None], grouped[:, local_cols], 0.0)
            result = block_apply(
                inverse, precondition_vector - couple(jacobian, precondition_picked)
            )
        search.append(result)
        whole = gathered_by_axis(result, GRP_BLK, (0, 2, 3, 1), 1)
        picked = whole[:, block_cols]
        image = couple(jacobian, picked)
        partial_value = jnp.stack([jnp.sum(basis_vec * image) for basis_vec in basis])
        projections, squares = (
            by_axis(partial_value, GRP_BLK),
            by_axis(jnp.sum(image * image), GRP_BLK),
        )
        for index_i, basis_vec in enumerate(basis):
            image = image - projections[index_i] * basis_vec
        length = jnp.sqrt(squares - jnp.sum(projections * projections) + EPS)
        hess = hess.at[: krylov_step + 1, krylov_step].set(projections)
        hess = hess.at[krylov_step + 1, krylov_step].set(length)
        if krylov_step + 1 < KRYLOV:
            basis.append(image / length)
    normal = jnp.dot(hess.T, hess, precision=lax.Precision.HIGHEST)
    coef = solve_small(normal, beta * hess[0])
    update = coef[0] * search[0]
    for index_j in range(1, KRYLOV):
        update = update + coef[index_j] * search[index_j]
    return (update, jacobian, beta * search[0])


def solution(mesh):
    torus = Mesh(mesh.devices.reshape(4, 2, 4, 4), ("grp_0", "grp_1", "blk_0", "blk_1"))
    return jax.shard_map(
        local,
        mesh=torus,
        in_specs=(
            P(GRP_BLK, None, None, None),
            P(GRP_BLK, None, None),
            P(GRP_BLK, None),
            P(None, GRP_BLK),
            P(None, GRP_BLK),
            P(None, GRP_BLK),
        ),
        out_specs=(P(None, GRP_BLK), P(None, None, None, GRP_BLK), P(None, GRP_BLK)),
        check_vma=False,
    )
```

profile of v0, /device:TPU:2, one launch (start us, length us, event | category | flops | bytes accessed | tf_op | source)
XLA Modules:
  0.0 1031.7 jit_solution(8667777961732287962)
XLA Ops:
  28.3 9.4 psum.308
  43.7 10.9 %psum.310 = f32[]{:T(128)} all-reduce(f32[]{:T(128)} %psum.309), channel_id=1, replica_groups=mesh['grp_0'=4,'grp_1'=2,'blk_0'=4,'blk_1'=4] {'blk_0'}, use_global_device_ids=true, to_apply=%region_3.4 | all-reduce | flops 1 | bytes 8 | tf_op jit(solution)/shard_map/psum | solution.py:70
  56.9 11.8 %psum.311 = f32[]{:T(128)} all-reduce(f32[]{:T(128)} %psum.310), channel_id=1, replica_groups=mesh['grp_0'=4,'grp_1'=2,'blk_0'=4,'blk_1'=4] {'blk_1'}, use_global_device_ids=true, to_apply=%region_4.5 | all-reduce | flops 1 | bytes 8 | tf_op jit(solution)/shard_map/psum | solution.py:70
  77.9 17.9 %all-to-all-done.1 = f32[128,1,2048]{2,1,0:T(1,128)S(1)} async-done(((f32[128,1,2048]{2,1,0:T(1,128)}), f32[128,1,2048]{2,1,0:T(1,128)S(1)}, u32[]{:S(2)}, u32[]{:S(2)}) %all-to-all-start.1) | async-done | bytes 1048608 | tf_op jit(solution)/shard_map/all_to_all | solution.py:135
  102.8 23.6 %scatter_custom_fusion.1 = f32[4096,64]{1,0:T(8,128)S(1)} fusion(s32[4096]{0:T(1024)S(1)} %reshape.1985, f32[4096,64]{1,0:T(8,128)} %bitcast.629, f32[]{:T(128)} %constant.944.clone.1), kind=kCustom, calls=%fused_computation.43 | custom fusion | flops 262144 | bytes 1049088
  126.4 9.9 scatter_fusion
  150.7 14.1 %gather_fusion = f32[4096,8]{1,0:T(8,128)} fusion(f32[8,4096]{0,1:T(8,128)S(1)} %bitcast.604, s32[4096]{0:T(1024)S(1)} %broadcast_clamp_fusion.1), kind=kCustom, calls=%fused_computation | custom fusion | bytes 278528 | tf_op jit(solution)/shard_map/gather | solution.py:180
  167.5 11.3 %all_to_all.71 = f32[16,8,256]{2,1,0:T(8,128)S(1)} all-to-all(f32[16,8,256]{2,1,0:T(8,128)S(1)} %broadcast_in_dim.117), channel_id=1, replica_groups=mesh['grp_0'=4,'grp_1'=2,'blk_0'=4,'blk_1'=4] {'blk_0','blk_1'}, dimensions={0} | all-to-all | bytes 262144 | tf_op jit(solution)/shard_map/all_to_all | solution.py:45
  179.4 14.1 %gather_fusion.1 = f32[4096,8]{1,0:T(8,128)} fusion(f32[8,4096]{0,1:T(8,128)S(1)} %bitcast.605, s32[4096]{0:T(1024)S(1)} %broadcast_clamp_fusion.1), kind=kCustom, calls=%fused_computation.1 | custom fusion | bytes 278528 | tf_op jit(solution)/shard_map/gather | solution.py:180
  196.1 11.3 %all-gather = f32[32,256]{1,0:T(8,128)S(1)} all-gather(f32[8,256]{1,0:T(8,128)S(1)} %bitcast.658), channel_id=2, replica_groups=mesh['grp_0'=4,'grp_1'=2,'blk_0'=4,'blk_1'=4] {'grp_0'}, dimensions={0}, use_global_device_ids=true | all-gather | bytes 40960 | tf_op jit(solution)/shard_map/all_gather | solution.py:57
  207.4 12.0 %all_gather.61 = f32[16,8,256]{2,1,0:T(8,128)S(1)} all-gather(f32[4,8,256]{2,1,0:T(8,128)S(1)} %bitcast.653), channel_id=1, replica_groups=mesh['grp_0'=4,'grp_1'=2,'blk_0'=4,'blk_1'=4] {'blk_0'}, dimensions={0}, use_global_device_ids=true | all-gather | bytes 163840 | tf_op jit(solution)/shard_map/all_gather | solution.py:57
  219.4 13.5 %all_gather.62 = f32[64,8,256]{2,1,0:T(8,128)} all-gather(f32[16,8,256]{2,1,0:T(8,128)S(1)} %all_gather.61), channel_id=1, replica_groups=mesh['grp_0'=4,'grp_1'=2,'blk_0'=4,'blk_1'=4] {'blk_1'}, dimensions={0}, use_global_device_ids=true | all-gather | bytes 655360 | tf_op jit(solution)/shard_map/all_gather | solution.py:57
  233.0 9.8 all-gather.11.cloned.1.call-done
  242.8 9.8 copy.83
  252.6 16.5 %gather_fusion.2 = f32[4096,8]{1,0:T(8,128)S(1)} fusion(f32[8,32768]{0,1:T(8,128)} %bitcast.597, s32[4096]{0:T(1024)S(1)} %broadcast_clamp_fusion), kind=kCustom, calls=%fused_computation.2 | custom fusion | bytes 278528 | tf_op jit(solution)/shard_map/gather | solution.py:186
  270.5 9.2 all-reduce.15
  282.7 11.1 %all-reduce.10 = (f32[1]{0:T(128)}, f32[]{:T(128)}) all-reduce(f32[1]{0:T(128)} %get-tuple-element.481, f32[]{:T(128)} %get-tuple-element.482), channel_id=1, replica_groups=mesh['grp_0'=4,'grp_1'=2,'blk_0'=4,'blk_1'=4] {'blk_0'}, use_global_device_ids=true, to_apply=%region_10.11 | all-reduce | flops 2 | bytes 16 | tf_op jit(solution)/shard_map/psum | solution.py:70
  293.8 11.3 %all-reduce.5 = (f32[1]{0:T(128)}, f32[]{:T(128)}) all-reduce(f32[1]{0:T(128)} %get-tuple-element.461, f32[]{:T(128)} %get-tuple-element.462), channel_id=1, replica_groups=mesh['grp_0'=4,'grp_1'=2,'blk_0'=4,'blk_1'=4] {'blk_1'}, use_global_device_ids=true, to_apply=%region_11.12 | all-reduce | flops 2 | bytes 16 | tf_op jit(solution)/shard_map/psum | solution.py:70
  307.8 10.4 %all_to_all.72 = f32[16,8,256]{2,1,0:T(8,128)S(1)} all-to-all(f32[16,8,256]{2,1,0:T(8,128)S(1)} %broadcast_in_dim.120), channel_id=1, replica_groups=mesh['grp_0'=4,'grp_1'=2,'blk_0'=4,'blk_1'=4] {'blk_0','blk_1'}, dimensions={0} | all-to-all | bytes 262144 | tf_op jit(solution)/shard_map/all_to_all | solution.py:45
  318.8 14.1 %gather_fusion.3 = f32[4096,8]{1,0:T(8,128)} fusion(f32[8,4096]{0,1:T(8,128)S(1)} %bitcast.606, s32[4096]{0:T(1024)S(1)} %broadcast_clamp_fusion.1), kind=kCustom, calls=%fused_computation.3 | custom fusion | bytes 278528 | tf_op jit(solution)/shard_map/gather | solution.py:180
  335.6 11.3 %all_to_all.73 = f32[16,8,256]{2,1,0:T(8,128)S(1)} all-to-all(f32[16,8,256]{2,1,0:T(8,128)S(1)} %broadcast_in_dim.121), channel_id=1, replica_groups=mesh['grp_0'=4,'grp_1'=2,'blk_0'=4,'blk_1'=4] {'blk_0','blk_1'}, dimensions={0} | all-to-all | bytes 262144 | tf_op jit(solution)/shard_map/all_to_all | solution.py:45
  347.5 14.1 %gather_fusion.4 = f32[4096,8]{1,0:T(8,128)} fusion(f32[8,4096]{0,1:T(8,128)S(1)} %bitcast.607, s32[4096]{0:T(1024)S(1)} %broadcast_clamp_fusion.1), kind=kCustom, calls=%fused_computation.4 | custom fusion | bytes 278528 | tf_op jit(solution)/shard_map/gather | solution.py:180
  364.2 11.1 %all-gather.1 = f32[32,256]{1,0:T(8,128)S(1)} all-gather(f32[8,256]{1,0:T(8,128)S(1)} %bitcast.659), channel_id=3, replica_groups=mesh['grp_0'=4,'grp_1'=2,'blk_0'=4,'blk_1'=4] {'grp_0'}, dimensions={0}, use_global_device_ids=true | all-gather | bytes 40960 | tf_op jit(solution)/shard_map/all_gather | solution.py:57
  375.3 12.0 %all_gather.65 = f32[16,8,256]{2,1,0:T(8,128)S(1)} all-gather(f32[4,8,256]{2,1,0:T(8,128)S(1)} %bitcast.654), channel_id=1, replica_groups=mesh['grp_0'=4,'grp_1'=2,'blk_0'=4,'blk_1'=4] {'blk_0'}, dimensions={0}, use_global_device_ids=true | all-gather | bytes 163840 | tf_op jit(solution)/shard_map/all_gather | solution.py:57
  387.3 13.5 %all_gather.66 = f32[64,8,256]{2,1,0:T(8,128)} all-gather(f32[16,8,256]{2,1,0:T(8,128)S(1)} %all_gather.65), channel_id=1, replica_groups=mesh['grp_0'=4,'grp_1'=2,'blk_0'=4,'blk_1'=4] {'blk_1'}, dimensions={0}, use_global_device_ids=true | all-gather | bytes 655360 | tf_op jit(solution)/shard_map/all_gather | solution.py:57
  400.9 11.1 %all-gather.13.cloned.1.call-done = f32[128,8,256]{2,1,0:T(8,128)} async-done(((f32[64,8,256]{2,1,0:T(8,128)}), f32[128,8,256]{2,1,0:T(8,128)}) %all-gather.13.cloned.1.call-update) | async-done | bytes 1048592 | tf_op jit(solution)/shard_map/all_gather | solution.py:57
  412.0 9.8 copy.86
  421.8 16.5 %gather_fusion.5 = f32[4096,8]{1,0:T(8,128)S(1)} fusion(f32[8,32768]{0,1:T(8,128)} %bitcast.598, s32[4096]{0:T(1024)S(1)} %broadcast_clamp_fusion), kind=kCustom, calls=%fused_computation.5 | custom fusion | bytes 278528 | tf_op jit(solution)/shard_map/gather | solution.py:186
  453.3 11.1 %all-reduce.9 = (f32[2]{0:T(128)S(1)}, f32[]{:T(128)}) all-reduce(f32[2]{0:T(128)S(1)} %get-tuple-element.479, f32[]{:T(128)} %get-tuple-element.480), channel_id=1, replica_groups=mesh['grp_0'=4,'grp_1'=2,'blk_0'=4,'blk_1'=4] {'blk_0'}, use_global_device_ids=true, to_apply=%region_22.23 | all-reduce | flops 3 | bytes 24 | tf_op jit(solution)/shard_map/psum | solution.py:70
  464.4 11.4 %all-reduce.4 = (f32[2]{0:T(128)S(1)}, f32[]{:T(128)}) all-reduce(f32[2]{0:T(128)S(1)} %get-tuple-element.459, f32[]{:T(128)} %get-tuple-element.460), channel_id=1, replica_groups=mesh['grp_0'=4,'grp_1'=2,'blk_0'=4,'blk_1'=4] {'blk_1'}, use_global_device_ids=true, to_apply=%region_23.24 | all-reduce | flops 3 | bytes 24 | tf_op jit(solution)/shard_map/psum | solution.py:70
  479.6 10.6 %all_to_all.74 = f32[16,8,256]{2,1,0:T(8,128)S(1)} all-to-all(f32[16,8,256]{2,1,0:T(8,128)S(1)} %broadcast_in_dim.123), channel_id=1, replica_groups=mesh['grp_0'=4,'grp_1'=2,'blk_0'=4,'blk_1'=4] {'blk_0','blk_1'}, dimensions={0} | all-to-all | bytes 262144 | tf_op jit(solution)/shard_map/all_to_all | solution.py:45
  490.8 14.1 %gather_fusion.6 = f32[4096,8]{1,0:T(8,128)} fusion(f32[8,4096]{0,1:T(8,128)S(1)} %bitcast.608, s32[4096]{0:T(1024)S(1)} %broadcast_clamp_fusion.1), kind=kCustom, calls=%fused_computation.6 | custom fusion | bytes 278528 | tf_op jit(solution)/shard_map/gather | solution.py:180
  507.6 11.3 %all_to_all.75 = f32[16,8,256]{2,1,0:T(8,128)S(1)} all-to-all(f32[16,8,256]{2,1,0:T(8,128)S(1)} %broadcast_in_dim.124), channel_id=1, replica_groups=mesh['grp_0'=4,'grp_1'=2,'blk_0'=4,'blk_1'=4] {'blk_0','blk_1'}, dimensions={0} | all-to-all | bytes 262144 | tf_op jit(solution)/shard_map/all_to_all | solution.py:45
  519.5 14.1 %gather_fusion.7 = f32[4096,8]{1,0:T(8,128)} fusion(f32[8,4096]{0,1:T(8,128)S(1)} %bitcast.609, s32[4096]{0:T(1024)S(1)} %broadcast_clamp_fusion.1), kind=kCustom, calls=%fused_computation.7 | custom fusion | bytes 278528 | tf_op jit(solution)/shard_map/gather | solution.py:180
  536.2 11.1 %all-gather.2 = f32[32,256]{1,0:T(8,128)S(1)} all-gather(f32[8,256]{1,0:T(8,128)S(1)} %bitcast.660), channel_id=4, replica_groups=mesh['grp_0'=4,'grp_1'=2,'blk_0'=4,'blk_1'=4] {'grp_0'}, dimensions={0}, use_global_device_ids=true | all-gather | bytes 40960 | tf_op jit(solution)/shard_map/all_gather | solution.py:57
  547.3 12.0 %all_gather.69 = f32[16,8,256]{2,1,0:T(8,128)S(1)} all-gather(f32[4,8,256]{2,1,0:T(8,128)S(1)} %bitcast.655), channel_id=1, replica_groups=mesh['grp_0'=4,'grp_1'=2,'blk_0'=4,'blk_1'=4] {'blk_0'}, dimensions={0}, use_global_device_ids=true | all-gather | bytes 163840 | tf_op jit(solution)/shard_map/all_gather | solution.py:57
  559.3 13.5 %all_gather.70 = f32[64,8,256]{2,1,0:T(8,128)} all-gather(f32[16,8,256]{2,1,0:T(8,128)S(1)} %all_gather.69), channel_id=1, replica_groups=mesh['grp_0'=4,'grp_1'=2,'blk_0'=4,'blk_1'=4] {'blk_1'}, dimensions={0}, use_global_device_ids=true | all-gather | bytes 655360 | tf_op jit(solution)/shard_map/all_gather | solution.py:57
  572.9 11.1 %all-gather.15.cloned.1.call-done = f32[128,8,256]{2,1,0:T(8,128)} async-done(((f32[64,8,256]{2,1,0:T(8,128)}), f32[128,8,256]{2,1,0:T(8,128)}) %all-gather.15.cloned.1.call-update) | async-done | bytes 1048592 | tf_op jit(solution)/shard_map/all_gather | solution.py:57
  583.9 9.8 copy.89
  593.8 16.5 %gather_fusion.8 = f32[4096,8]{1,0:T(8,128)S(1)} fusion(f32[8,32768]{0,1:T(8,128)} %bitcast.599, s32[4096]{0:T(1024)S(1)} %broadcast_clamp_fusion), kind=kCustom, calls=%fused_computation.8 | custom fusion | bytes 278528 | tf_op jit(solution)/shard_map/gather | solution.py:186
  625.9 11.1 %all-reduce.8 = (f32[3]{0:T(128)S(1)}, f32[]{:T(128)}) all-reduce(f32[3]{0:T(128)S(1)} %get-tuple-element.477, f32[]{:T(128)} %get-tuple-element.478), channel_id=1, replica_groups=mesh['grp_0'=4,'grp_1'=2,'blk_0'=4,'blk_1'=4] {'blk_0'}, use_global_device_ids=true, to_apply=%region_36.37 | all-reduce | flops 4 | bytes 32 | tf_op jit(solution)/shard_map/psum | solution.py:70
  637.0 11.4 %all-reduce.3 = (f32[3]{0:T(128)S(1)}, f32[]{:T(128)}) all-reduce(f32[3]{0:T(128)S(1)} %get-tuple-element.457, f32[]{:T(128)} %get-tuple-element.458), channel_id=1, replica_groups=mesh['grp_0'=4,'grp_1'=2,'blk_0'=4,'blk_1'=4] {'blk_1'}, use_global_device_ids=true, to_apply=%region_37.38 | all-reduce | flops 4 | bytes 32 | tf_op jit(solution)/shard_map/psum | solution.py:70
  652.9 10.4 %all_to_all.76 = f32[16,8,256]{2,1,0:T(8,128)S(1)} all-to-all(f32[16,8,256]{2,1,0:T(8,128)S(1)} %broadcast_in_dim.126), channel_id=1, replica_groups=mesh['grp_0'=4,'grp_1'=2,'blk_0'=4,'blk_1'=4] {'blk_0','blk_1'}, dimensions={0} | all-to-all | bytes 262144 | tf_op jit(solution)/shard_map/all_to_all | solution.py:45
  663.9 14.1 %gather_fusion.9 = f32[4096,8]{1,0:T(8,128)} fusion(f32[8,4096]{0,1:T(8,128)S(1)} %bitcast.610, s32[4096]{0:T(1024)S(1)} %broadcast_clamp_fusion.1), kind=kCustom, calls=%fused_computation.9 | custom fusion | bytes 278528 | tf_op jit(solution)/shard_map/gather | solution.py:180
  680.7 11.3 %all_to_all.77 = f32[16,8,256]{2,1,0:T(8,128)S(1)} all-to-all(f32[16,8,256]{2,1,0:T(8,128)S(1)} %broadcast_in_dim.127), channel_id=1, replica_groups=mesh['grp_0'=4,'grp_1'=2,'blk_0'=4,'blk_1'=4] {'blk_0','blk_1'}, dimensions={0} | all-to-all | bytes 262144 | tf_op jit(solution)/shard_map/all_to_all | solution.py:45
  692.5 14.1 %gather_fusion.10 = f32[4096,8]{1,0:T(8,128)} fusion(f32[8,4096]{0,1:T(8,128)S(1)} %bitcast.611, s32[4096]{0:T(1024)S(1)} %broadcast_clamp_fusion.1), kind=kCustom, calls=%fused_computation.10 | custom fusion | bytes 278528 | tf_op jit(solution)/shard_map/gather | solution.py:180
  709.3 11.1 %all-gather.3 = f32[32,256]{1,0:T(8,128)S(1)} all-gather(f32[8,256]{1,0:T(8,128)S(1)} %bitcast.661), channel_id=5, replica_groups=mesh['grp_0'=4,'grp_1'=2,'blk_0'=4,'blk_1'=4] {'grp_0'}, dimensions={0}, use_global_device_ids=true | all-gather | bytes 40960 | tf_op jit(solution)/shard_map/all_gather | solution.py:57
  720.4 12.0 %all_gather.73 = f32[16,8,256]{2,1,0:T(8,128)S(1)} all-gather(f32[4,8,256]{2,1,0:T(8,128)S(1)} %bitcast.656), channel_id=1, replica_groups=mesh['grp_0'=4,'grp_1'=2,'blk_0'=4,'blk_1'=4] {'blk_0'}, dimensions={0}, use_global_device_ids=true | all-gather | bytes 163840 | tf_op jit(solution)/shard_map/all_gather | solution.py:57
  732.3 13.5 %all_gather.74 = f32[64,8,256]{2,1,0:T(8,128)} all-gather(f32[16,8,256]{2,1,0:T(8,128)S(1)} %all_gather.73), channel_id=1, replica_groups=mesh['grp_0'=4,'grp_1'=2,'blk_0'=4,'blk_1'=4] {'blk_1'}, dimensions={0}, use_global_device_ids=true | all-gather | bytes 655360 | tf_op jit(solution)/shard_map/all_gather | solution.py:57
  746.6 10.5 %all-gather.17.cloned.1.call-done = f32[128,8,256]{2,1,0:T(8,128)} async-done(((f32[64,8,256]{2,1,0:T(8,128)}), f32[128,8,256]{2,1,0:T(8,128)}) %all-gather.17.cloned.1.call-update) | async-done | bytes 1048592 | tf_op jit(solution)/shard_map/all_gather | solution.py:57
  757.0 9.8 copy.92
  766.8 16.5 %gather_fusion.11 = f32[4096,8]{1,0:T(8,128)S(1)} fusion(f32[8,32768]{0,1:T(8,128)} %bitcast.600, s32[4096]{0:T(1024)S(1)} %broadcast_clamp_fusion), kind=kCustom, calls=%fused_computation.11 | custom fusion | bytes 278528 | tf_op jit(solution)/shard_map/gather | solution.py:186
  799.6 11.1 %all-reduce.7 = (f32[4]{0:T(128)S(1)}, f32[]{:T(128)}) all-reduce(f32[4]{0:T(128)S(1)} %get-tuple-element.475, f32[]{:T(128)} %get-tuple-element.476), channel_id=1, replica_groups=mesh['grp_0'=4,'grp_1'=2,'blk_0'=4,'blk_1'=4] {'blk_0'}, use_global_device_ids=true, to_apply=%region_51.52 | all-reduce | flops 5 | bytes 40 | tf_op jit(solution)/shard_map/psum | solution.py:70
  810.7 11.3 %all-reduce.2 = (f32[4]{0:T(128)S(1)}, f32[]{:T(128)}) all-reduce(f32[4]{0:T(128)S(1)} %get-tuple-element.455, f32[]{:T(128)} %get-tuple-element.456), channel_id=1, replica_groups=mesh['grp_0'=4,'grp_1'=2,'blk_0'=4,'blk_1'=4] {'blk_1'}, use_global_device_ids=true, to_apply=%region_52.53 | all-reduce | flops 5 | bytes 40 | tf_op jit(solution)/shard_map/psum | solution.py:70
  839.6 14.1 %gather_fusion.12 = f32[4096,8]{1,0:T(8,128)} fusion(f32[8,4096]{0,1:T(8,128)S(1)} %bitcast.612, s32[4096]{0:T(1024)S(1)} %broadcast_clamp_fusion.1), kind=kCustom, calls=%fused_computation.12 | custom fusion | bytes 278528 | tf_op jit(solution)/shard_map/gather | solution.py:180
  869.1 14.1 %gather_fusion.13 = f32[4096,8]{1,0:T(8,128)} fusion(f32[8,4096]{0,1:T(8,128)S(1)} %bitcast.603, s32[4096]{0:T(1024)S(1)} %broadcast_clamp_fusion.1), kind=kCustom, calls=%fused_computation.13 | custom fusion | bytes 278528 | tf_op jit(solution)/shard_map/gather | solution.py:180
  885.9 11.1 %all-gather.4 = f32[32,256]{1,0:T(8,128)S(1)} all-gather(f32[8,256]{1,0:T(8,128)S(1)} %bitcast.662), channel_id=6, replica_groups=mesh['grp_0'=4,'grp_1'=2,'blk_0'=4,'blk_1'=4] {'grp_0'}, dimensions={0}, use_global_device_ids=true | all-gather | bytes 40960 | tf_op jit(solution)/shard_map/all_gather | solution.py:57
  897.0 12.0 %all_gather.77 = f32[16,8,256]{2,1,0:T(8,128)S(1)} all-gather(f32[4,8,256]{2,1,0:T(8,128)S(1)} %bitcast.657), channel_id=1, replica_groups=mesh['grp_0'=4,'grp_1'=2,'blk_0'=4,'blk_1'=4] {'blk_0'}, dimensions={0}, use_global_device_ids=true | all-gather | bytes 163840 | tf_op jit(solution)/shard_map/all_gather | solution.py:57
  909.0 13.5 %all_gather.78 = f32[64,8,256]{2,1,0:T(8,128)} all-gather(f32[16,8,256]{2,1,0:T(8,128)S(1)} %all_gather.77), channel_id=1, replica_groups=mesh['grp_0'=4,'grp_1'=2,'blk_0'=4,'blk_1'=4] {'blk_1'}, dimensions={0}, use_global_device_ids=true | all-gather | bytes 655360 | tf_op jit(solution)/shard_map/all_gather | solution.py:57
  937.1 9.8 copy.95
  947.0 16.5 %gather_fusion.14 = f32[4096,8]{1,0:T(8,128)S(1)} fusion(f32[8,32768]{0,1:T(8,128)} %bitcast.596, s32[4096]{0:T(1024)S(1)} %broadcast_clamp_fusion), kind=kCustom, calls=%fused_computation.14 | custom fusion | bytes 278528 | tf_op jit(solution)/shard_map/gather | solution.py:186
  968.1 11.6 %all-reduce.11 = (f32[5]{0:T(128)S(1)}, f32[]{:T(128)}) all-reduce(f32[5]{0:T(128)S(1)} %stack.120, f32[]{:T(128)} %get-tuple-element.423), channel_id=1, replica_groups=mesh['grp_0'=4,'grp_1'=2,'blk_0'=4,'blk_1'=4] {'grp_0'}, use_global_device_ids=true, to_apply=%region_65.66 | all-reduce | flops 6 | bytes 48 | tf_op jit(solution)/shard_map/psum | solution.py:70
  982.7 9.5 all-reduce.6
  992.2 9.4 all-reduce.1
  (320 shorter events, 214.2 us)
Async XLA Ops:
  8.5 60.9 %collective-permute-start.1 = (s32[1]{0:T(128)}, s32[1]{0:T(128)}, u32[]{:S(2)}, u32[]{:S(2)}) collective-permute-start(s32[1]{0:T(128)} %bitcast.71), channel_id=1, source_target_pairs={{127,0},{0,1},{1,2},{2,3},{3,4},{4,5},{5,6},{6,7},{7,8},{8,9},{9,1... | collective-permute-start | bytes 20 | tf_op jit(solution)/shard_map/ppermute | solution.py:34
  11.3 66.4 %collective-permute-start.2 = (f32[64,96]{1,0:T(8,128)S(1)}, f32[64,96]{1,0:T(8,128)S(1)}, u32[]{:S(2)}, u32[]{:S(2)}) collective-permute-start(f32[64,96]{1,0:T(8,128)S(1)} %slice.984), channel_id=1, source_target_pairs={{127,0},{0,1},{1,2},{2,3},{3,4},{4,5},{5,6},{6,7},{7,8},{8,9},{9,1... | collective-permute-start | bytes 73736 | tf_op jit(solution)/shard_map/ppermute | solution.py:34
  14.1 56.9 %collective-permute-start = (s32[96]{0:T(128)S(1)}, s32[96]{0:T(128)S(1)}, u32[]{:S(2)}, u32[]{:S(2)}) collective-permute-start(s32[96]{0:T(128)S(1)} %slice_bitcast_fusion.6), channel_id=1, source_target_pairs={{127,0},{0,1},{1,2},{2,3},{3,4},{4,5},{5,6},{6,7},{7,8},{8,9},{9,1... | collective-permute-start | bytes 1160 | tf_op jit(solution)/shard_map/ppermute | solution.py:34
  18.0 53.0 %all-to-all-start = ((s32[1,128,33]{2,0,1:T(1,128)}), s32[1,128,33]{2,0,1:T(1,128)S(1)}, u32[]{:S(2)}, u32[]{:S(2)}) async-start(s32[1,128,33]{2,0,1:T(1,128)} %copy.71), calls=%async_computation | async-start | bytes 131072 | tf_op jit(solution)/shard_map/all_to_all | solution.py:20
  43.6 25.7 %copy-start.1 = (f32[8,256]{1,0:T(8,128)S(1)}, f32[8,256]{1,0:T(8,128)}, u32[]{:S(2)}) copy-start(f32[8,256]{1,0:T(8,128)} %param.81) | copy-start | bytes 24580
  43.6 25.8 %copy-start.3 = (s32[16,256]{1,0:T(8,128)S(1)}, s32[16,256]{1,0:T(8,128)}, u32[]{:S(2)}) copy-start(s32[16,256]{1,0:T(8,128)} %param.80) | copy-start | bytes 49156
  56.8 20.3 %copy-start.5 = (s32[2]{0:T(128)S(1)}, s32[2]{0:T(128)}, u32[]{:S(2)}) copy-start(s32[2]{0:T(128)} %constant.981) | copy-start | bytes 28
  56.8 20.4 %copy-start.4 = (s32[2]{0:T(128)S(1)}, s32[2]{0:T(128)}, u32[]{:S(2)}) copy-start(s32[2]{0:T(128)} %constant.984) | copy-start | bytes 28
  71.1 24.8 %all-to-all-start.1 = ((f32[128,1,2048]{2,1,0:T(1,128)}), f32[128,1,2048]{2,1,0:T(1,128)S(1)}, u32[]{:S(2)}, u32[]{:S(2)}) async-start(f32[128,1,2048]{2,1,0:T(1,128)} %reshape.2102), calls=%async_computation.1 | async-start | bytes 2097152 | tf_op jit(solution)/shard_map/all_to_all | solution.py:135
  136.3 0.7 copy-start.2
  137.2 826.8 %copy-start = (f32[16,8,8,256]{3,2,1,0:T(8,128)}, f32[16,8,8,256]{3,2,1,0:T(8,128)S(1)}, u32[]{:S(2)}) copy-start(f32[16,8,8,256]{3,2,1,0:T(8,128)S(1)} %get-tuple-element.493) | copy-start | bytes 3145732
  138.8 11.3 %all-to-all-start.2 = ((f32[16,8,256]{2,1,0:T(8,128)}), f32[16,8,256]{2,1,0:T(8,128)S(1)}, u32[]{:S(2)}, u32[]{:S(2)}) async-start(f32[16,8,256]{2,1,0:T(8,128)} %broadcast_in_dim.114), calls=%async_computation.2 | async-start | bytes 262144 | tf_op jit(solution)/shard_map/all_to_all | solution.py:45
  142.3 100.5 %all-gather.11.cloned.1.call-start = ((), (), s32[]{:S(2)}) async-start(), calls=%async_computation.12 | async-start | bytes 1572864 | tf_op jit(solution)/shard_map/all_gather | solution.py:57
  232.9 179.0 %all-gather.13.cloned.1.call-start = ((), (), s32[]{:S(2)}) async-start(), calls=%async_computation.13 | async-start | bytes 1572864 | tf_op jit(solution)/shard_map/all_gather | solution.py:57
  400.8 183.1 %all-gather.15.cloned.1.call-start = ((), (), s32[]{:S(2)}) async-start(), calls=%async_computation.14 | async-start | bytes 1572864 | tf_op jit(solution)/shard_map/all_gather | solution.py:57
  572.8 184.2 %all-gather.17.cloned.1.call-start = ((), (), s32[]{:S(2)}) async-start(), calls=%async_computation.15 | async-start | bytes 1572864 | tf_op jit(solution)/shard_map/all_gather | solution.py:57
  827.7 11.3 %all-to-all-start.10 = ((f32[16,8,256]{2,1,0:T(8,128)}), f32[16,8,256]{2,1,0:T(8,128)S(1)}, u32[]{:S(2)}, u32[]{:S(2)}) async-start(f32[16,8,256]{2,1,0:T(8,128)} %broadcast_in_dim.129), calls=%async_computation.10 | async-start | bytes 262144 | tf_op jit(solution)/shard_map/all_to_all | solution.py:45
  857.0 11.5 %all-to-all-start.11 = ((f32[16,8,256]{2,1,0:T(8,128)}), f32[16,8,256]{2,1,0:T(8,128)S(1)}, u32[]{:S(2)}, u32[]{:S(2)}) async-start(f32[16,8,256]{2,1,0:T(8,128)} %broadcast_in_dim.130), calls=%async_computation.11 | async-start | bytes 262144 | tf_op jit(solution)/shard_map/all_to_all | solution.py:45
  860.7 76.4 %all-gather.19.cloned.1.call-start = ((), (), s32[]{:S(2)}) async-start(), calls=%async_computation.16 | async-start | bytes 1572864 | tf_op jit(solution)/shard_map/all_gather | solution.py:57
  885.1 38.7 %copy-start.8 = (s32[2]{0:T(128)S(1)}, s32[2]{0:T(128)}, u32[]{:S(2)}) copy-start(s32[2]{0:T(128)} %constant.972.clone.1) | copy-start | bytes 28
  885.2 39.3 %copy-start.7 = (s32[2]{0:T(128)S(1)}, s32[2]{0:T(128)}, u32[]{:S(2)}) copy-start(s32[2]{0:T(128)} %constant.973.clone.1) | copy-start | bytes 28
  885.2 40.1 %copy-start.6 = (s32[2]{0:T(128)S(1)}, s32[2]{0:T(128)}, u32[]{:S(2)}) copy-start(s32[2]{0:T(128)} %constant.974.clone.1) | copy-start | bytes 28
Sparse Core Ops, SparseCore 0:
  233.1 9.6 all-gather.10
  400.9 10.9 all-gather.12
  572.9 10.9 all-gather.14
  746.0 10.9 all-gather.16
  922.6 10.9 all-gather.18
where the time goes:
time: 1040 us; the launch traced here: 1030 us
  blocking collectives  467 us (45%)
  local copies, waits for them, and re-layouts  323 us (31%)
  other arithmetic  97.5 us (9%)
  waiting for transfers between devices  82.3 us (8%)
  starting transfers between devices  31.2 us (3%)
  between operations  30.1 us (3%)
    psum x24, blocking collectives, by_axis(): array = lax.psum(array, axis)  208 us
    all_gather x15, blocking collectives, all_blocks(): parts = lax.all_gather(parts, axes[k], axis=0, tiled=True)  183 us
    gather x10, local copies, waits for them, and re-layouts, local(): precondition_picked = jnp.where(near[None], grouped[:, local_cols], 0.0)  141 us
    gather x5, local copies, waits for them, and re-layouts, local(): picked = whole[:, block_cols]  82.7 us
    all_to_all x7, blocking collectives, copy_for_each(): lax.all_to_all(jnp.broadcast_to(array[None], (length, *array.shape)), axi...  76.5 us
    transpose x5, local copies, waits for them, and re-layouts, all_blocks(): parts.transpose(*turned, *range(len(sequence), parts.ndim))  49.1 us
    unnamed x26, other arithmetic  43.2 us
    all_gather x5, waiting for transfers between devices, all_blocks(): parts = lax.all_gather(parts, axes[k], axis=0, tiled=True)  42.4 us
  transfers between devices with their start and end apart: 13, of which 8 were waited for; matrix products, arithmetic and copies ran while one was open for 3% of the time, Pallas kernels for 0%

commit v1 on v0

--- a/solution.py
+++ b/solution.py
@@ -13,6 +13,14 @@
 EPS = 1e-06
 
 
+def _list_clusters(x_local, link_axis):
+    wide_out = tuple((x_local for _ in range(lax.psum(1, axis_name=link_axis))))
+    t_next = jnp.stack(wide_out, axis=0)
+    return jnp.concatenate(
+        lax.all_to_all(t_next, axis_name=link_axis, split_axis=0, concat_axis=0), axis=0
+    )
+
+
 def sent_together(arrays, axis, split_dim, concat_dim, along):
     columns = [a.reshape(*a.shape[:along], -1) for a in arrays]
     both = jnp.concatenate(columns, axis=along)
@@ -54,7 +62,7 @@
 def all_blocks(array, axes, sequence):
     parts = array[None]
     for k in sequence:
-        parts = lax.all_gather(parts, axes[k], axis=0, tiled=True)
+        parts = _list_clusters(parts, axes[k])
     held = [lax.axis_size(axes[k]) for k in reversed(sequence)]
     parts = parts.reshape(*held, *array.shape)
     turned = sorted(range(len(sequence)), key=lambda place: sequence[len(sequence) - 1 - place])

time: 1040 us -> 937 us (0.901)
  blocking collectives: 467 us -> 372 us
  starting transfers between devices: 31.2 us -> 52.4 us
  waiting for transfers between devices: 82.3 us -> 64.9 us
  between operations: 30.1 us -> 17.2 us
    all_gather x15 -> x0, blocking collectives: 183 us -> none  [all_blocks(): parts = lax.all_gather(parts, axes[k], axis=0, tiled=True)]
    all_to_all x0 -> x14, blocking collectives: none -> 99.5 us  [_list_clusters(): lax.all_to_all(t_next, axis_name=link_axis, split_axis=0, concat_axis=0)]
    transpose x5, local copies, waits for them, and re-layouts: 49.1 us -> 0.63 us  [all_blocks(): parts.transpose(*turned, *range(len(sequence), parts.ndim))]
    all_gather x5 -> x0, waiting for transfers between devices: 42.4 us -> none  [all_blocks(): parts = lax.all_gather(parts, axes[k], axis=0, tiled=True)]
    transpose x10 -> x15, local copies, waits for them, and re-layouts: 5.97 us -> 47.4 us  [in_order(): return jnp.moveaxis(parts, 0, dim).reshape(dims)]
    all_to_all x0 -> x6, waiting for transfers between devices: none -> 25.5 us  [_list_clusters(): lax.all_to_all(t_next, axis_name=link_axis, split_axis=0, concat_axis=0)]
    all_to_all x0 -> x6, starting transfers between devices: none -> 21.5 us  [_list_clusters(): lax.all_to_all(t_next, axis_name=link_axis, split_axis=0, concat_axis=0)]
    psum x24, blocking collectives: 208 us -> 196 us  [by_axis(): array = lax.psum(array, axis)]
  transfers between devices with their start and end apart: 13 -> 14, of which waited for: 8 -> 10; matrix products, arithmetic and copies ran while one was open for 3% -> 3% of each run, Pallas kernels for 0% -> 0%
where the time goes in v1:
time: 937 us; the launch traced here: 925 us
  blocking collectives  372 us (40%)
  local copies, waits for them, and re-layouts  321 us (34%)
  other arithmetic  97.5 us (10%)
  waiting for transfers between devices  64.9 us (7%)
  starting transfers between devices  52.4 us (6%)
  between operations  17.2 us (2%)
    psum x24, blocking collectives, by_axis(): array = lax.psum(array, axis)  196 us
    gather x10, local copies, waits for them, and re-layouts, local(): precondition_picked = jnp.where(near[None], grouped[:, local_cols], 0.0)  141 us
    all_to_all x14, blocking collectives, _list_clusters(): lax.all_to_all(t_next, axis_name=link_axis, split_axis=0, concat_axis=0)  99.5 us
    gather x5, local copies, waits for them, and re-layouts, local(): picked = whole[:, block_cols]  82.7 us
    all_to_all x7, blocking collectives, copy_for_each(): lax.all_to_all(jnp.broadcast_to(array[None], (length, *array.shape)), axi...  76.3 us
    transpose x15, local copies, waits for them, and re-layouts, in_order(): return jnp.moveaxis(parts, 0, dim).reshape(dims)  47.4 us
    unnamed x26, other arithmetic  43.2 us
    all_to_all x6, waiting for transfers between devices, _list_clusters(): lax.all_to_all(t_next, axis_name=link_axis, split_axis=0, concat_axis=0)  25.5 us
  transfers between devices with their start and end apart: 14, of which 10 were waited for; matrix products, arithmetic and copies ran while one was open for 3% of the time, Pallas kernels for 0%

profile of v1, /device:TPU:2, one launch (start us, length us, event | category | flops | bytes accessed | tf_op | source)
XLA Modules:
  0.0 924.9 jit_solution(3027230983793422690)
XLA Ops:
  11.5 8.8 all-to-all-start
  21.8 9.4 %psum.308 = f32[]{:T(128)} all-reduce(f32[]{:T(128)} %multiply_reduce_fusion.31), channel_id=1, replica_groups=mesh['grp_0'=4,'grp_1'=2,'blk_0'=4,'blk_1'=4] {'grp_0'}, use_global_device_ids=true, to_apply=%region_1.2 | all-reduce | flops 1 | bytes 8 | tf_op jit(solution)/shard_map/psum | solution.py:78
  37.1 10.9 %psum.310 = f32[]{:T(128)} all-reduce(f32[]{:T(128)} %psum.309), channel_id=1, replica_groups=mesh['grp_0'=4,'grp_1'=2,'blk_0'=4,'blk_1'=4] {'blk_0'}, use_global_device_ids=true, to_apply=%region_3.4 | all-reduce | flops 1 | bytes 8 | tf_op jit(solution)/shard_map/psum | solution.py:78
  50.3 11.8 %psum.311 = f32[]{:T(128)} all-reduce(f32[]{:T(128)} %psum.310), channel_id=1, replica_groups=mesh['grp_0'=4,'grp_1'=2,'blk_0'=4,'blk_1'=4] {'blk_1'}, use_global_device_ids=true, to_apply=%region_4.5 | all-reduce | flops 1 | bytes 8 | tf_op jit(solution)/shard_map/psum | solution.py:78
  71.3 17.9 %all-to-all-done.1 = f32[128,1,2048]{2,1,0:T(1,128)S(1)} async-done(((f32[128,1,2048]{2,1,0:T(1,128)}), f32[128,1,2048]{2,1,0:T(1,128)S(1)}, u32[]{:S(2)}, u32[]{:S(2)}) %all-to-all-start.1) | async-done | bytes 1048608 | tf_op jit(solution)/shard_map/all_to_all | solution.py:143
  96.3 23.6 %scatter_custom_fusion.1 = f32[4096,64]{1,0:T(8,128)S(1)} fusion(s32[4096]{0:T(1024)S(1)} %reshape.1995, f32[4096,64]{1,0:T(8,128)} %bitcast.649, f32[]{:T(128)} %constant.944.clone.1), kind=kCustom, calls=%fused_computation.48 | custom fusion | flops 262144 | bytes 1049088
  119.9 9.9 %scatter_fusion = f32[16,64,256]{1,2,0:T(8,128)S(1)} fusion(f32[16,64,256]{1,2,0:T(8,128)S(1)} %bitcast.606, s32[192]{0:T(256)S(1)} %reshape.1989, f32[192,64]{1,0:T(8,128)S(1)} %bitcast.671), kind=kCustom, calls=%fused_computation.15 | custom fusion | flops 12288 | bytes 148992 | tf_op jit(solution)/shard_map/scatter-add | solution.py:131
  135.9 7.7 all-to-all-done.2
  144.2 14.1 %gather_fusion = f32[4096,8]{1,0:T(8,128)} fusion(f32[8,4096]{0,1:T(8,128)S(1)} %bitcast.609, s32[4096]{0:T(1024)S(1)} %broadcast_clamp_fusion.1), kind=kCustom, calls=%fused_computation | custom fusion | bytes 278528 | tf_op jit(solution)/shard_map/gather | solution.py:188
  161.0 11.3 %all_to_all.171 = f32[16,8,256]{2,1,0:T(8,128)S(1)} all-to-all(f32[16,8,256]{2,1,0:T(8,128)S(1)} %broadcast_in_dim.107), channel_id=1, replica_groups=mesh['grp_0'=4,'grp_1'=2,'blk_0'=4,'blk_1'=4] {'blk_0','blk_1'}, dimensions={0} | all-to-all | bytes 262144 | tf_op jit(solution)/shard_map/all_to_all | solution.py:53
  172.8 14.1 %gather_fusion.1 = f32[4096,8]{1,0:T(8,128)} fusion(f32[8,4096]{0,1:T(8,128)S(1)} %bitcast.610, s32[4096]{0:T(1024)S(1)} %broadcast_clamp_fusion.1), kind=kCustom, calls=%fused_computation.1 | custom fusion | bytes 278528 | tf_op jit(solution)/shard_map/gather | solution.py:188
  189.6 7.7 all_to_all.172
  197.3 8.4 all_to_all.173
  210.0 8.0 all-to-all-done.6
  222.8 8.3 copy.84
  231.1 16.5 %gather_fusion.2 = f32[4096,8]{1,0:T(8,128)S(1)} fusion(f32[8,32768]{0,1:T(8,128)} %bitcast.602, s32[4096]{0:T(1024)S(1)} %broadcast_clamp_fusion), kind=kCustom, calls=%fused_computation.2 | custom fusion | bytes 278528 | tf_op jit(solution)/shard_map/gather | solution.py:194
  248.9 9.8 %all-reduce.15 = (f32[1]{0:T(128)}, f32[]{:T(128)}) all-reduce(f32[1]{0:T(128)} %bitcast.134, f32[]{:T(128)} %get-tuple-element.441), channel_id=1, replica_groups=mesh['grp_0'=4,'grp_1'=2,'blk_0'=4,'blk_1'=4] {'grp_0'}, use_global_device_ids=true, to_apply=%region_8.9 | all-reduce | flops 2 | bytes 16 | tf_op jit(solution)/shard_map/psum | solution.py:78
  261.8 9.5 %all-reduce.10 = (f32[1]{0:T(128)}, f32[]{:T(128)}) all-reduce(f32[1]{0:T(128)} %get-tuple-element.481, f32[]{:T(128)} %get-tuple-element.482), channel_id=1, replica_groups=mesh['grp_0'=4,'grp_1'=2,'blk_0'=4,'blk_1'=4] {'blk_0'}, use_global_device_ids=true, to_apply=%region_10.11 | all-reduce | flops 2 | bytes 16 | tf_op jit(solution)/shard_map/psum | solution.py:78
  271.3 9.5 %all-reduce.5 = (f32[1]{0:T(128)}, f32[]{:T(128)}) all-reduce(f32[1]{0:T(128)} %get-tuple-element.461, f32[]{:T(128)} %get-tuple-element.462), channel_id=1, replica_groups=mesh['grp_0'=4,'grp_1'=2,'blk_0'=4,'blk_1'=4] {'blk_1'}, use_global_device_ids=true, to_apply=%region_11.12 | all-reduce | flops 2 | bytes 16 | tf_op jit(solution)/shard_map/psum | solution.py:78
  283.5 10.4 %all_to_all.175 = f32[16,8,256]{2,1,0:T(8,128)S(1)} all-to-all(f32[16,8,256]{2,1,0:T(8,128)S(1)} %broadcast_in_dim.109), channel_id=1, replica_groups=mesh['grp_0'=4,'grp_1'=2,'blk_0'=4,'blk_1'=4] {'blk_0','blk_1'}, dimensions={0} | all-to-all | bytes 262144 | tf_op jit(solution)/shard_map/all_to_all | solution.py:53
  294.5 14.1 %gather_fusion.3 = f32[4096,8]{1,0:T(8,128)} fusion(f32[8,4096]{0,1:T(8,128)S(1)} %bitcast.611, s32[4096]{0:T(1024)S(1)} %broadcast_clamp_fusion.1), kind=kCustom, calls=%fused_computation.3 | custom fusion | bytes 278528 | tf_op jit(solution)/shard_map/gather | solution.py:188
  311.3 11.3 %all_to_all.176 = f32[16,8,256]{2,1,0:T(8,128)S(1)} all-to-all(f32[16,8,256]{2,1,0:T(8,128)S(1)} %broadcast_in_dim.110), channel_id=1, replica_groups=mesh['grp_0'=4,'grp_1'=2,'blk_0'=4,'blk_1'=4] {'blk_0','blk_1'}, dimensions={0} | all-to-all | bytes 262144 | tf_op jit(solution)/shard_map/all_to_all | solution.py:53
  323.2 14.1 %gather_fusion.4 = f32[4096,8]{1,0:T(8,128)} fusion(f32[8,4096]{0,1:T(8,128)S(1)} %bitcast.612, s32[4096]{0:T(1024)S(1)} %broadcast_clamp_fusion.1), kind=kCustom, calls=%fused_computation.4 | custom fusion | bytes 278528 | tf_op jit(solution)/shard_map/gather | solution.py:188
  339.9 7.5 all_to_all.177
  347.5 8.4 all_to_all.178
  355.9 10.7 %all_to_all.179 = f32[4,16,8,256]{3,2,1,0:T(8,128)S(1)} all-to-all(f32[4,16,8,256]{3,2,1,0:T(8,128)S(1)} %stack.169), channel_id=1, replica_groups=mesh['grp_0'=4,'grp_1'=2,'blk_0'=4,'blk_1'=4] {'blk_1'}, dimensions={0} | all-to-all | bytes 1048576 | tf_op jit(solution)/shard_map/all_to_all | solution.py:20
  371.3 8.3 copy.88
  379.6 16.5 %gather_fusion.5 = f32[4096,8]{1,0:T(8,128)S(1)} fusion(f32[8,32768]{0,1:T(8,128)} %bitcast.603, s32[4096]{0:T(1024)S(1)} %broadcast_clamp_fusion), kind=kCustom, calls=%fused_computation.5 | custom fusion | bytes 278528 | tf_op jit(solution)/shard_map/gather | solution.py:194
  398.8 9.8 %all-reduce.14 = (f32[2]{0:T(128)S(1)}, f32[]{:T(128)}) all-reduce(f32[2]{0:T(128)S(1)} %pad_maximum_fusion.5, f32[]{:T(128)} %get-tuple-element.438), channel_id=1, replica_groups=mesh['grp_0'=4,'grp_1'=2,'blk_0'=4,'blk_1'=4] {'grp_0'}, use_global_device_ids=true, to_apply=%region_20.21 | all-reduce | flops 3 | bytes 24 | tf_op jit(solution)/shard_map/psum | solution.py:78
  411.7 9.5 %all-reduce.9 = (f32[2]{0:T(128)S(1)}, f32[]{:T(128)}) all-reduce(f32[2]{0:T(128)S(1)} %get-tuple-element.479, f32[]{:T(128)} %get-tuple-element.480), channel_id=1, replica_groups=mesh['grp_0'=4,'grp_1'=2,'blk_0'=4,'blk_1'=4] {'blk_0'}, use_global_device_ids=true, to_apply=%region_22.23 | all-reduce | flops 3 | bytes 24 | tf_op jit(solution)/shard_map/psum | solution.py:78
  421.2 9.8 %all-reduce.4 = (f32[2]{0:T(128)S(1)}, f32[]{:T(128)}) all-reduce(f32[2]{0:T(128)S(1)} %get-tuple-element.459, f32[]{:T(128)} %get-tuple-element.460), channel_id=1, replica_groups=mesh['grp_0'=4,'grp_1'=2,'blk_0'=4,'blk_1'=4] {'blk_1'}, use_global_device_ids=true, to_apply=%region_23.24 | all-reduce | flops 3 | bytes 24 | tf_op jit(solution)/shard_map/psum | solution.py:78
  434.9 10.4 %all_to_all.181 = f32[16,8,256]{2,1,0:T(8,128)S(1)} all-to-all(f32[16,8,256]{2,1,0:T(8,128)S(1)} %broadcast_in_dim.111), channel_id=1, replica_groups=mesh['grp_0'=4,'grp_1'=2,'blk_0'=4,'blk_1'=4] {'blk_0','blk_1'}, dimensions={0} | all-to-all | bytes 262144 | tf_op jit(solution)/shard_map/all_to_all | solution.py:53
  445.9 14.1 %gather_fusion.6 = f32[4096,8]{1,0:T(8,128)} fusion(f32[8,4096]{0,1:T(8,128)S(1)} %bitcast.613, s32[4096]{0:T(1024)S(1)} %broadcast_clamp_fusion.1), kind=kCustom, calls=%fused_computation.6 | custom fusion | bytes 278528 | tf_op jit(solution)/shard_map/gather | solution.py:188
  462.7 11.3 %all_to_all.182 = f32[16,8,256]{2,1,0:T(8,128)S(1)} all-to-all(f32[16,8,256]{2,1,0:T(8,128)S(1)} %broadcast_in_dim.112), channel_id=1, replica_groups=mesh['grp_0'=4,'grp_1'=2,'blk_0'=4,'blk_1'=4] {'blk_0','blk_1'}, dimensions={0} | all-to-all | bytes 262144 | tf_op jit(solution)/shard_map/all_to_all | solution.py:53
  474.5 14.1 %gather_fusion.7 = f32[4096,8]{1,0:T(8,128)} fusion(f32[8,4096]{0,1:T(8,128)S(1)} %bitcast.614, s32[4096]{0:T(1024)S(1)} %broadcast_clamp_fusion.1), kind=kCustom, calls=%fused_computation.7 | custom fusion | bytes 278528 | tf_op jit(solution)/shard_map/gather | solution.py:188
  491.3 7.5 all_to_all.183
  498.8 8.4 all_to_all.184
  507.2 10.7 %all_to_all.185 = f32[4,16,8,256]{3,2,1,0:T(8,128)S(1)} all-to-all(f32[4,16,8,256]{3,2,1,0:T(8,128)S(1)} %stack.176), channel_id=1, replica_groups=mesh['grp_0'=4,'grp_1'=2,'blk_0'=4,'blk_1'=4] {'blk_1'}, dimensions={0} | all-to-all | bytes 1048576 | tf_op jit(solution)/shard_map/all_to_all | solution.py:20
  522.7 8.3 copy.92
  531.0 16.5 %gather_fusion.8 = f32[4096,8]{1,0:T(8,128)S(1)} fusion(f32[8,32768]{0,1:T(8,128)} %bitcast.604, s32[4096]{0:T(1024)S(1)} %broadcast_clamp_fusion), kind=kCustom, calls=%fused_computation.8 | custom fusion | bytes 278528 | tf_op jit(solution)/shard_map/gather | solution.py:194
  550.8 9.8 %all-reduce.13 = (f32[3]{0:T(128)S(1)}, f32[]{:T(128)}) all-reduce(f32[3]{0:T(128)S(1)} %pad_maximum_fusion.6, f32[]{:T(128)} %get-tuple-element.434), channel_id=1, replica_groups=mesh['grp_0'=4,'grp_1'=2,'blk_0'=4,'blk_1'=4] {'grp_0'}, use_global_device_ids=true, to_apply=%region_34.35 | all-reduce | flops 4 | bytes 32 | tf_op jit(solution)/shard_map/psum | solution.py:78
  563.7 9.5 %all-reduce.8 = (f32[3]{0:T(128)S(1)}, f32[]{:T(128)}) all-reduce(f32[3]{0:T(128)S(1)} %get-tuple-element.477, f32[]{:T(128)} %get-tuple-element.478), channel_id=1, replica_groups=mesh['grp_0'=4,'grp_1'=2,'blk_0'=4,'blk_1'=4] {'blk_0'}, use_global_device_ids=true, to_apply=%region_36.37 | all-reduce | flops 4 | bytes 32 | tf_op jit(solution)/shard_map/psum | solution.py:78
  573.2 9.6 %all-reduce.3 = (f32[3]{0:T(128)S(1)}, f32[]{:T(128)}) all-reduce(f32[3]{0:T(128)S(1)} %get-tuple-element.457, f32[]{:T(128)} %get-tuple-element.458), channel_id=1, replica_groups=mesh['grp_0'=4,'grp_1'=2,'blk_0'=4,'blk_1'=4] {'blk_1'}, use_global_device_ids=true, to_apply=%region_37.38 | all-reduce | flops 4 | bytes 32 | tf_op jit(solution)/shard_map/psum | solution.py:78
  587.3 10.4 %all_to_all.187 = f32[16,8,256]{2,1,0:T(8,128)S(1)} all-to-all(f32[16,8,256]{2,1,0:T(8,128)S(1)} %broadcast_in_dim.113), channel_id=1, replica_groups=mesh['grp_0'=4,'grp_1'=2,'blk_0'=4,'blk_1'=4] {'blk_0','blk_1'}, dimensions={0} | all-to-all | bytes 262144 | tf_op jit(solution)/shard_map/all_to_all | solution.py:53
  598.3 14.1 %gather_fusion.9 = f32[4096,8]{1,0:T(8,128)} fusion(f32[8,4096]{0,1:T(8,128)S(1)} %bitcast.615, s32[4096]{0:T(1024)S(1)} %broadcast_clamp_fusion.1), kind=kCustom, calls=%fused_computation.9 | custom fusion | bytes 278528 | tf_op jit(solution)/shard_map/gather | solution.py:188
  615.1 11.3 %all_to_all.188 = f32[16,8,256]{2,1,0:T(8,128)S(1)} all-to-all(f32[16,8,256]{2,1,0:T(8,128)S(1)} %broadcast_in_dim.114), channel_id=1, replica_groups=mesh['grp_0'=4,'grp_1'=2,'blk_0'=4,'blk_1'=4] {'blk_0','blk_1'}, dimensions={0} | all-to-all | bytes 262144 | tf_op jit(solution)/shard_map/all_to_all | solution.py:53
  627.0 14.1 %gather_fusion.10 = f32[4096,8]{1,0:T(8,128)} fusion(f32[8,4096]{0,1:T(8,128)S(1)} %bitcast.616, s32[4096]{0:T(1024)S(1)} %broadcast_clamp_fusion.1), kind=kCustom, calls=%fused_computation.10 | custom fusion | bytes 278528 | tf_op jit(solution)/shard_map/gather | solution.py:188
  643.8 7.5 all_to_all.189
  655.3 5.9 all-to-all-done.23
  667.4 6.1 all-to-all-done.24
  678.3 8.3 copy.96
  686.6 16.5 %gather_fusion.11 = f32[4096,8]{1,0:T(8,128)S(1)} fusion(f32[8,32768]{0,1:T(8,128)} %bitcast.605, s32[4096]{0:T(1024)S(1)} %broadcast_clamp_fusion), kind=kCustom, calls=%fused_computation.11 | custom fusion | bytes 278528 | tf_op jit(solution)/shard_map/gather | solution.py:194
  707.0 9.8 %all-reduce.12 = (f32[4]{0:T(128)S(1)}, f32[]{:T(128)}) all-reduce(f32[4]{0:T(128)S(1)} %pad_maximum_fusion.7, f32[]{:T(128)} %get-tuple-element.429), channel_id=1, replica_groups=mesh['grp_0'=4,'grp_1'=2,'blk_0'=4,'blk_1'=4] {'grp_0'}, use_global_device_ids=true, to_apply=%region_49.50 | all-reduce | flops 5 | bytes 40 | tf_op jit(solution)/shard_map/psum | solution.py:78
  720.0 9.5 %all-reduce.7 = (f32[4]{0:T(128)S(1)}, f32[]{:T(128)}) all-reduce(f32[4]{0:T(128)S(1)} %get-tuple-element.475, f32[]{:T(128)} %get-tuple-element.476), channel_id=1, replica_groups=mesh['grp_0'=4,'grp_1'=2,'blk_0'=4,'blk_1'=4] {'blk_0'}, use_global_device_ids=true, to_apply=%region_51.52 | all-reduce | flops 5 | bytes 40 | tf_op jit(solution)/shard_map/psum | solution.py:78
  729.5 9.5 %all-reduce.2 = (f32[4]{0:T(128)S(1)}, f32[]{:T(128)}) all-reduce(f32[4]{0:T(128)S(1)} %get-tuple-element.455, f32[]{:T(128)} %get-tuple-element.456), channel_id=1, replica_groups=mesh['grp_0'=4,'grp_1'=2,'blk_0'=4,'blk_1'=4] {'blk_1'}, use_global_device_ids=true, to_apply=%region_52.53 | all-reduce | flops 5 | bytes 40 | tf_op jit(solution)/shard_map/psum | solution.py:78
  749.7 6.5 all-to-all-done.26
  756.8 14.1 %gather_fusion.12 = f32[4096,8]{1,0:T(8,128)} fusion(f32[8,4096]{0,1:T(8,128)S(1)} %bitcast.617, s32[4096]{0:T(1024)S(1)} %broadcast_clamp_fusion.1), kind=kCustom, calls=%fused_computation.12 | custom fusion | bytes 278528 | tf_op jit(solution)/shard_map/gather | solution.py:188
  778.6 7.2 all-to-all-done.27
  786.3 14.1 %gather_fusion.13 = f32[4096,8]{1,0:T(8,128)} fusion(f32[8,4096]{0,1:T(8,128)S(1)} %bitcast.608, s32[4096]{0:T(1024)S(1)} %broadcast_clamp_fusion.1), kind=kCustom, calls=%fused_computation.13 | custom fusion | bytes 278528 | tf_op jit(solution)/shard_map/gather | solution.py:188
  839.2 8.3 copy.100
  847.4 16.5 %gather_fusion.14 = f32[4096,8]{1,0:T(8,128)S(1)} fusion(f32[8,32768]{0,1:T(8,128)} %bitcast.601, s32[4096]{0:T(1024)S(1)} %broadcast_clamp_fusion), kind=kCustom, calls=%fused_computation.14 | custom fusion | bytes 278528 | tf_op jit(solution)/shard_map/gather | solution.py:194
  868.6 9.8 %all-reduce.11 = (f32[5]{0:T(128)S(1)}, f32[]{:T(128)}) all-reduce(f32[5]{0:T(128)S(1)} %stack.200, f32[]{:T(128)} %get-tuple-element.423), channel_id=1, replica_groups=mesh['grp_0'=4,'grp_1'=2,'blk_0'=4,'blk_1'=4] {'grp_0'}, use_global_device_ids=true, to_apply=%region_65.66 | all-reduce | flops 6 | bytes 48 | tf_op jit(solution)/shard_map/psum | solution.py:78
  881.5 9.5 %all-reduce.6 = (f32[5]{0:T(128)S(1)}, f32[]{:T(128)}) all-reduce(f32[5]{0:T(128)S(1)} %get-tuple-element.473, f32[]{:T(128)} %get-tuple-element.474), channel_id=1, replica_groups=mesh['grp_0'=4,'grp_1'=2,'blk_0'=4,'blk_1'=4] {'blk_0'}, use_global_device_ids=true, to_apply=%region_67.68 | all-reduce | flops 6 | bytes 48 | tf_op jit(solution)/shard_map/psum | solution.py:78
  891.0 10.4 %all-reduce.1 = (f32[5]{0:T(128)S(1)}, f32[]{:T(128)}) all-reduce(f32[5]{0:T(128)S(1)} %get-tuple-element.453, f32[]{:T(128)} %get-tuple-element.454), channel_id=1, replica_groups=mesh['grp_0'=4,'grp_1'=2,'blk_0'=4,'blk_1'=4] {'blk_1'}, use_global_device_ids=true, to_apply=%region_68.69 | all-reduce | flops 6 | bytes 48 | tf_op jit(solution)/shard_map/psum | solution.py:78
  (341 shorter events, 210.7 us)
Async XLA Ops:
  2.0 60.9 %collective-permute-start.1 = (s32[1]{0:T(128)}, s32[1]{0:T(128)}, u32[]{:S(2)}, u32[]{:S(2)}) collective-permute-start(s32[1]{0:T(128)} %bitcast.71), channel_id=1, source_target_pairs={{127,0},{0,1},{1,2},{2,3},{3,4},{4,5},{5,6},{6,7},{7,8},{8,9},{9,1... | collective-permute-start | bytes 20 | tf_op jit(solution)/shard_map/ppermute | solution.py:42
  4.8 66.4 %collective-permute-start.2 = (f32[64,96]{1,0:T(8,128)S(1)}, f32[64,96]{1,0:T(8,128)S(1)}, u32[]{:S(2)}, u32[]{:S(2)}) collective-permute-start(f32[64,96]{1,0:T(8,128)S(1)} %slice.984), channel_id=1, source_target_pairs={{127,0},{0,1},{1,2},{2,3},{3,4},{4,5},{5,6},{6,7},{7,8},{8,9},{9,1... | collective-permute-start | bytes 73736 | tf_op jit(solution)/shard_map/ppermute | solution.py:42
  7.5 56.9 %collective-permute-start = (s32[96]{0:T(128)S(1)}, s32[96]{0:T(128)S(1)}, u32[]{:S(2)}, u32[]{:S(2)}) collective-permute-start(s32[96]{0:T(128)S(1)} %slice_bitcast_fusion.6), channel_id=1, source_target_pairs={{127,0},{0,1},{1,2},{2,3},{3,4},{4,5},{5,6},{6,7},{7,8},{8,9},{9,1... | collective-permute-start | bytes 1160 | tf_op jit(solution)/shard_map/ppermute | solution.py:42
  11.5 53.0 %all-to-all-start = ((s32[1,128,33]{2,0,1:T(1,128)}), s32[1,128,33]{2,0,1:T(1,128)S(1)}, u32[]{:S(2)}, u32[]{:S(2)}) async-start(s32[1,128,33]{2,0,1:T(1,128)} %copy.71), calls=%async_computation | async-start | bytes 131072 | tf_op jit(solution)/shard_map/all_to_all | solution.py:28
  37.1 25.7 %copy-start.1 = (f32[8,256]{1,0:T(8,128)S(1)}, f32[8,256]{1,0:T(8,128)}, u32[]{:S(2)}) copy-start(f32[8,256]{1,0:T(8,128)} %param.81) | copy-start | bytes 24580
  37.1 25.8 %copy-start.3 = (s32[16,256]{1,0:T(8,128)S(1)}, s32[16,256]{1,0:T(8,128)}, u32[]{:S(2)}) copy-start(s32[16,256]{1,0:T(8,128)} %param.80) | copy-start | bytes 49156
  50.3 20.3 %copy-start.5 = (s32[2]{0:T(128)S(1)}, s32[2]{0:T(128)}, u32[]{:S(2)}) copy-start(s32[2]{0:T(128)} %constant.981) | copy-start | bytes 28
  50.3 20.4 %copy-start.4 = (s32[2]{0:T(128)S(1)}, s32[2]{0:T(128)}, u32[]{:S(2)}) copy-start(s32[2]{0:T(128)} %constant.984) | copy-start | bytes 28
  64.5 24.8 %all-to-all-start.1 = ((f32[128,1,2048]{2,1,0:T(1,128)}), f32[128,1,2048]{2,1,0:T(1,128)S(1)}, u32[]{:S(2)}, u32[]{:S(2)}) async-start(f32[128,1,2048]{2,1,0:T(1,128)} %reshape.2107), calls=%async_computation.1 | async-start | bytes 2097152 | tf_op jit(solution)/shard_map/all_to_all | solution.py:143
  129.8 0.7 copy-start.2
  130.7 733.8 %copy-start = (f32[16,8,8,256]{3,2,1,0:T(8,128)}, f32[16,8,8,256]{3,2,1,0:T(8,128)S(1)}, u32[]{:S(2)}) copy-start(f32[16,8,8,256]{3,2,1,0:T(8,128)S(1)} %get-tuple-element.493) | copy-start | bytes 3145732
  132.3 11.3 %all-to-all-start.2 = ((f32[16,8,256]{2,1,0:T(8,128)}), f32[16,8,256]{2,1,0:T(8,128)S(1)}, u32[]{:S(2)}, u32[]{:S(2)}) async-start(f32[16,8,256]{2,1,0:T(8,128)} %broadcast_in_dim.104), calls=%async_computation.2 | async-start | bytes 262144 | tf_op jit(solution)/shard_map/all_to_all | solution.py:53
  206.5 11.5 %all-to-all-start.6 = ((f32[4,16,8,256]{3,2,1,0:T(8,128)}), f32[4,16,8,256]{3,2,1,0:T(8,128)S(1)}, u32[]{:S(2)}, u32[]{:S(2)}) async-start(f32[4,16,8,256]{3,2,1,0:T(8,128)} %stack.164), calls=%async_computation.6 | async-start | bytes 1048576 | tf_op jit(solution)/shard_map/all_to_all | solution.py:20
  643.6 23.2 %copy-start.8 = (s32[2]{0:T(128)S(1)}, s32[2]{0:T(128)}, u32[]{:S(2)}) copy-start(s32[2]{0:T(128)} %constant.972.clone.1) | copy-start | bytes 28
  651.9 9.3 %all-to-all-start.23 = ((f32[4,4,8,256]{3,2,1,0:T(8,128)}), f32[4,4,8,256]{3,2,1,0:T(8,128)S(1)}, u32[]{:S(2)}, u32[]{:S(2)}) async-start(f32[4,4,8,256]{3,2,1,0:T(8,128)} %stack.183), calls=%async_computation.23 | async-start | bytes 262144 | tf_op jit(solution)/shard_map/all_to_all | solution.py:20
  662.0 11.5 %all-to-all-start.24 = ((f32[4,16,8,256]{3,2,1,0:T(8,128)}), f32[4,16,8,256]{3,2,1,0:T(8,128)S(1)}, u32[]{:S(2)}, u32[]{:S(2)}) async-start(f32[4,16,8,256]{3,2,1,0:T(8,128)} %stack.184), calls=%async_computation.24 | async-start | bytes 1048576 | tf_op jit(solution)/shard_map/all_to_all | solution.py:20
  703.1 45.9 %copy-start.7 = (s32[2]{0:T(128)S(1)}, s32[2]{0:T(128)}, u32[]{:S(2)}) copy-start(s32[2]{0:T(128)} %constant.973.clone.1) | copy-start | bytes 28
  744.7 11.5 %all-to-all-start.26 = ((f32[16,8,256]{2,1,0:T(8,128)}), f32[16,8,256]{2,1,0:T(8,128)S(1)}, u32[]{:S(2)}, u32[]{:S(2)}) async-start(f32[16,8,256]{2,1,0:T(8,128)} %broadcast_in_dim.115), calls=%async_computation.26 | async-start | bytes 262144 | tf_op jit(solution)/shard_map/all_to_all | solution.py:53
  772.9 5.0 copy-start.6
  774.3 11.5 %all-to-all-start.27 = ((f32[16,8,256]{2,1,0:T(8,128)}), f32[16,8,256]{2,1,0:T(8,128)S(1)}, u32[]{:S(2)}, u32[]{:S(2)}) async-start(f32[16,8,256]{2,1,0:T(8,128)} %broadcast_in_dim.116), calls=%async_computation.27 | async-start | bytes 262144 | tf_op jit(solution)/shard_map/all_to_all | solution.py:53
  803.7 8.4 all-to-all-start.28
  812.8 9.3 %all-to-all-start.29 = ((f32[4,4,8,256]{3,2,1,0:T(8,128)}), f32[4,4,8,256]{3,2,1,0:T(8,128)S(1)}, u32[]{:S(2)}, u32[]{:S(2)}) async-start(f32[4,4,8,256]{3,2,1,0:T(8,128)} %stack.192), calls=%async_computation.29 | async-start | bytes 262144 | tf_op jit(solution)/shard_map/all_to_all | solution.py:20
  822.9 11.5 %all-to-all-start.30 = ((f32[4,16,8,256]{3,2,1,0:T(8,128)}), f32[4,16,8,256]{3,2,1,0:T(8,128)S(1)}, u32[]{:S(2)}, u32[]{:S(2)}) async-start(f32[4,16,8,256]{3,2,1,0:T(8,128)} %stack.193), calls=%async_computation.30 | async-start | bytes 1048576 | tf_op jit(solution)/shard_map/all_to_all | solution.py:20
